TPU v7x, 512 devices: a whole 4x4x16 slice. The times are simulated.
512 devices in a mesh: tm: 32 (over y, x, core), stream: 16 (over z).
Axes of the slice: x: 4, y: 4, z: 16, core: 2. Of those that a mesh axis runs over, the one named last changes fastest.
Arguments:
- tokens: bfloat16 [65536, 2048], P(('tm', 'stream')), may hold values from -6 to 6
- w_query: bfloat16 [2048, 2048], P('stream'), may hold values from -0.125 to 0.125
- w_key: bfloat16 [2048, 2048], P('stream'), may hold values from -0.125 to 0.125
- w_value: bfloat16 [2048, 2048], P('stream'), may hold values from -0.125 to 0.125
- decay_proj: bfloat16 [2048, 16], P('stream'), may hold values from -0.125 to 0.125
- beta_proj: bfloat16 [2048, 16], P('stream'), may hold values from -0.125 to 0.125
- decay_rate: float32 [16], replicated, may hold values from 1.5258789e-05 to 0.1
- beta_bias: float32 [16], replicated, may hold values from -7 to 0
- norm_gain: float32 [128], replicated, may hold values from 0.5 to 1.5
Outputs:
- mixed: bfloat16 [65536, 2048], P(('tm', 'stream'))
All inputs are finite; a program needn't handle non-finite values.
Results may differ from a plain program's by a relative error of at most 0.0073.
Values may be sent and summed in bfloat16 or wider, within the bound.
No kernel may reach another device: no remote copies, remote signals or barrier semaphores. Data moves between devices by JAX's collectives and lax.ppermute only.
A program may use at most 128 MiB of HBM per device.

v0:
```python
import jax
import jax.numpy as jnp
from jax import lax
from jax.sharding import Mesh
from jax.sharding import PartitionSpec as P

HEADS = 16
DK = 128
DV = 128
GROUP = 256
TM = ("tm_0", "tm_1", "tm_2")
TM_STREAM = ("tm_0", "tm_1", "tm_2", "stream")
highest_precision = lax.Precision.HIGHEST


def in_one_piece(arrays, axis, dim, along):
    widths = [a.shape[along] for a in arrays]
    both = jnp.concatenate(arrays, axis=along)
    whole = lax.all_gather(both, axis, axis=dim, tiled=True)
    return tuple(jnp.split(whole, [sum(widths[:k]) for k in range(1, len(widths))], axis=along))


def nothing_yet(x, identity):
    return jax.tree.map(
        lambda a, e: jnp.broadcast_to(jnp.asarray(e, a.dtype), a.shape), x, identity
    )


def carried_in(x, axes, combine, identity):
    before = start = nothing_yet(x, identity)
    subtotal = x
    for axis in reversed(axes):
        length, place = (lax.axis_size(axis), lax.axis_index(axis))
        pieces = jax.tree.map(lambda part: lax.all_gather(part, axis), subtotal)
        inside, subtotal = (start, start)
        for k in range(length):
            passed = k < place
            subtotal = combine(subtotal, jax.tree.map(lambda part: part[k], pieces))
            inside = jax.tree.map(lambda new, old: jnp.where(passed, new, old), subtotal, inside)
        before = combine(inside, before)
    return before


def add_rows(inputs, piece):
    return jnp.dot(inputs, piece, preferred_element_type=jnp.float32)


def compose_pairs(earlier, later):
    first_map, first_shift = earlier
    second_map, second_shift = later
    joined_map = jnp.einsum("udf,ufe->ude", first_map, second_map, precision=highest_precision)
    joined_shift = (
        jnp.einsum("ued,udf->uef", first_shift, second_map, precision=highest_precision)
        + second_shift
    )
    return (joined_map, joined_shift)


def shards(
    tokens, w_query, w_key, w_value, decay_proj, beta_proj, decay_rate, beta_bias, norm_gain
):
    local_rows = tokens.shape[0]
    streams = lax.axis_size("stream")
    per_device = HEADS // streams

    def fold_one(piece):
        return add_rows(tokens, piece)

    raw_query = fold_one(lax.all_gather(w_query, "stream", axis=0, tiled=True))
    raw_key = fold_one(lax.all_gather(w_key, "stream", axis=0, tiled=True))
    raw_value = fold_one(lax.all_gather(w_value, "stream", axis=0, tiled=True))
    pieces = in_one_piece((decay_proj, beta_proj), "stream", 0, 1)
    decay_logit, beta_logit = tuple((add_rows(tokens, piece) for piece in pieces))
    query_heads = raw_query.reshape(local_rows, HEADS, DK)
    key_heads = raw_key.reshape(local_rows, HEADS, DK)
    queries = (
        (
            query_heads
            * lax.rsqrt(jnp.sum(query_heads * query_heads, -1, keepdims=True) + 1e-06)
            * DK ** (-0.5)
        )
        .astype(jnp.bfloat16)
        .reshape(local_rows, HEADS * DK)
    )
    key_rows = (
        (key_heads * lax.rsqrt(jnp.sum(key_heads * key_heads, -1, keepdims=True) + 1e-06))
        .astype(jnp.bfloat16)
        .reshape(local_rows, HEADS * DK)
    )
    values = raw_value.astype(jnp.bfloat16)
    log_decay = (-decay_rate * jax.nn.softplus(decay_logit)).astype(jnp.bfloat16)
    strength = jax.nn.sigmoid(beta_logit + beta_bias).astype(jnp.bfloat16)
    got_query, got_key, got_value, got_decay, got_strength = (
        lax.all_to_all(queries, "stream", split_axis=1, concat_axis=0, tiled=True),
        lax.all_to_all(key_rows, "stream", split_axis=1, concat_axis=0, tiled=True),
        lax.all_to_all(values, "stream", split_axis=1, concat_axis=0, tiled=True),
        lax.all_to_all(log_decay, "stream", split_axis=1, concat_axis=0, tiled=True),
        lax.all_to_all(strength, "stream", split_axis=1, concat_axis=0, tiled=True),
    )
    block_rows = got_query.shape[0]
    num_blocks = block_rows // GROUP
    query_b = (
        got_query.reshape(num_blocks, GROUP, per_device, DK)
        .astype(jnp.float32)
        .transpose(0, 2, 1, 3)
    )
    key_b = (
        got_key.reshape(num_blocks, GROUP, per_device, DK).astype(jnp.float32).transpose(0, 2, 1, 3)
    )
    value_b = (
        got_value.reshape(num_blocks, GROUP, per_device, DV)
        .astype(jnp.float32)
        .transpose(0, 2, 1, 3)
    )
    decay_b = (
        got_decay.reshape(num_blocks, GROUP, per_device).astype(jnp.float32).transpose(0, 2, 1)
    )
    strength_b = (
        got_strength.reshape(num_blocks, GROUP, per_device).astype(jnp.float32).transpose(0, 2, 1)
    )
    positions = jnp.arange(GROUP)
    strict = positions[:, None] > positions[None, :]
    inclusive_mask = positions[:, None] >= positions[None, :]
    identity = jnp.eye(GROUP, dtype=jnp.float32)
    key_identity = jnp.eye(DK, dtype=jnp.float32)
    cumulative = jnp.cumsum(decay_b, axis=2)
    growth = jnp.exp(cumulative)
    last_log = cumulative[..., -1:]
    tail = jnp.exp(last_log - cumulative)
    key_products = jnp.einsum("nucd,numd->nucm", key_b, key_b, precision=highest_precision)
    spread = cumulative[..., :, None] - cumulative[..., None, :]
    decay_matrix = jnp.exp(jnp.where(inclusive_mask, spread, 0.0))
    lower = (
        jnp.where(strict, strength_b[..., :, None] * decay_matrix * key_products, 0.0) + identity
    )
    right_side = jnp.concatenate(
        [(strength_b * growth)[..., None] * key_b, strength_b[..., None] * value_b], -1
    )
    solved = jax.scipy.linalg.solve_triangular(lower, right_side, lower=True, unit_diagonal=True)
    weights_w = solved[..., :DK]
    updates = solved[..., DK:]
    key_tail = tail[..., None] * key_b
    attention_scores = jnp.where(
        inclusive_mask,
        jnp.einsum("nucd,numd->nucm", query_b, key_b, precision=highest_precision) * decay_matrix,
        0.0,
    )
    query_grown = growth[..., None] * query_b
    block_map = jnp.exp(last_log)[..., None] * key_identity - jnp.einsum(
        "nucd,nuce->nude", weights_w, key_tail, precision=highest_precision
    )
    block_shift = jnp.einsum("nuce,nucd->nued", updates, key_tail, precision=highest_precision)

    def compose_step(carry, pair):
        return (compose_pairs(carry, pair), carry)

    start_map = jnp.broadcast_to(key_identity, (per_device, DK, DK))
    start_shift = jnp.zeros((per_device, DV, DK), jnp.float32)
    totals, prefixes = lax.scan(compose_step, (start_map, start_shift), (block_map, block_shift))
    total_map, total_shift = totals
    prefix_map, prefix_shift = prefixes
    scanned = carried_in((total_map, total_shift), TM, compose_pairs, (start_map, start_shift))
    state_in = scanned[1]
    block_states = (
        jnp.einsum("ued,nudf->nuef", state_in, prefix_map, precision=highest_precision)
        + prefix_shift
    )
    fresh = updates - jnp.einsum(
        "nucd,nued->nuce", weights_w, block_states, precision=highest_precision
    )
    read = jnp.einsum(
        "nucd,nued->nuce", query_grown, block_states, precision=highest_precision
    ) + jnp.einsum("nucm,nume->nuce", attention_scores, fresh, precision=highest_precision)
    readout = read.transpose(0, 2, 1, 3).reshape(block_rows, per_device * DV).astype(jnp.bfloat16)
    returned = lax.all_to_all(readout, "stream", split_axis=0, concat_axis=1, tiled=True)
    head_read = returned.reshape(local_rows, HEADS, DV).astype(jnp.float32)
    normed = (
        head_read
        * lax.rsqrt(jnp.mean(head_read * head_read, -1, keepdims=True) + 1e-06)
        * norm_gain
    )
    return normed.reshape(local_rows, HEADS * DV).astype(jnp.bfloat16)


def solution(mesh):
    finer = Mesh(
        mesh.devices.reshape(4, 4, 2, mesh.shape["stream"]), ("tm_0", "tm_1", "tm_2", "stream")
    )
    return jax.shard_map(
        shards,
        mesh=finer,
        in_specs=(
            P(TM_STREAM, None),
            P("stream", None),
            P("stream", None),
            P("stream", None),
            P("stream", None),
            P("stream", None),
            P(),
            P(),
            P(),
        ),
        out_specs=P(TM_STREAM, None),
        check_vma=False,
    )
```

profile of v0, /device:TPU:34, one launch (start us, length us, event | category | flops | bytes accessed | tf_op | source)
XLA Modules:
  0.0 717.1 jit_solution(13404925184703037204)
XLA Ops:
  10.1 34.2 %all_gather.48 = bf16[2048,32]{0,1:T(8,128)(2,1)S(1)} all-gather(bf16[128,32]{0,1:T(8,128)(2,1)S(1)} %pad_maximum_fusion), channel_id=1, replica_groups=mesh['tm_0'=4,'tm_1'=4,'tm_2'=2,'stream'=16] {'stream'}, dimensions={0}, use_global_device_ids=true | all-gather | bytes 139264 | tf_op jit(solution)/shard_map/all_gather | solution.py:19
  45.2 9.1 %all-to-all-start = ((bf16[128,16,1]{0,2,1:T(2,128)(2,1)}), bf16[128,16,1]{0,2,1:T(2,128)(2,1)S(1)}, u32[]{:S(2)}, u32[]{:S(2)}) async-start(bf16[128,16,1]{0,2,1:T(2,128)(2,1)} %copy.65), calls=%async_computation | async-start | bytes 16384 | tf_op jit(solution)/shard_map/all_to_all | solution.py:97
  56.8 8.6 %all-to-all-done = bf16[128,16,1]{0,2,1:T(2,128)(2,1)S(1)} async-done(((bf16[128,16,1]{0,2,1:T(2,128)(2,1)}), bf16[128,16,1]{0,2,1:T(2,128)(2,1)S(1)}, u32[]{:S(2)}, u32[]{:S(2)}) %all-to-all-start) | async-done | bytes 4128 | tf_op jit(solution)/shard_map/all_to_all | solution.py:97
  65.4 4.6 all-to-all-start.2
  70.8 47.6 %all-gather.14.cloned.1.call-done = bf16[2048,2048]{1,0:T(8,128)(2,1)} async-done(((bf16[128,2048]{1,0:T(8,128)(2,1)}), bf16[2048,2048]{1,0:T(8,128)(2,1)}) %all-gather.14.cloned.1.call-update) | async-done | bytes 8388624 | tf_op jit(solution)/shard_map/all_gather | solution.py:71
  118.4 4.6 fusion.21
  124.0 11.4 %all-to-all-start.4 = ((bf16[128,16,128]{2,0,1:T(8,128)(2,1)}), bf16[128,16,128]{2,0,1:T(8,128)(2,1)S(1)}, u32[]{:S(2)}, u32[]{:S(2)}) async-start(bf16[128,16,128]{2,0,1:T(8,128)(2,1)} %bitcast.256), calls=%async_computation.4 | async-start | bytes 1048576 | tf_op jit(solution)/shard_map/all_to_all | solution.py:96
  135.6 109.5 %all-gather.12.cloned.1.call-done = bf16[2048,2048]{1,0:T(8,128)(2,1)} async-done(((bf16[128,2048]{1,0:T(8,128)(2,1)}), bf16[2048,2048]{1,0:T(8,128)(2,1)}) %all-gather.12.cloned.1.call-update) | async-done | bytes 8388624 | tf_op jit(solution)/shard_map/all_gather | solution.py:70
  245.0 4.6 fusion.143
  250.7 1.2 copy_bitcast_fusion.1
  251.9 11.1 %all-to-all-start.3 = ((bf16[128,16,128]{2,0,1:T(8,128)(2,1)}), bf16[128,16,128]{2,0,1:T(8,128)(2,1)S(1)}, u32[]{:S(2)}, u32[]{:S(2)}) async-start(bf16[128,16,128]{2,0,1:T(8,128)(2,1)} %copy_bitcast_fusion.1), calls=%async_computation.3 | async-start | bytes 1048576 | tf_op jit(solution)/shard_map/all_to_all | solution.py:95
  263.3 109.3 %all-gather.10.cloned.1.call-done = bf16[2048,2048]{1,0:T(8,128)(2,1)} async-done(((bf16[128,2048]{1,0:T(8,128)(2,1)}), bf16[2048,2048]{1,0:T(8,128)(2,1)}) %all-gather.10.cloned.1.call-update) | async-done | bytes 8388624 | tf_op jit(solution)/shard_map/all_gather | solution.py:69
  372.6 4.6 fusion.142
  378.3 1.2 copy_bitcast_fusion.2
  379.6 1.3 broadcast_multiply_fusion
  380.9 11.2 %all-to-all-start.1 = ((bf16[128,16,128]{2,0,1:T(8,128)(2,1)}), bf16[128,16,128]{2,0,1:T(8,128)(2,1)}, u32[]{:S(2)}, u32[]{:S(2)}) async-start(bf16[128,16,128]{2,0,1:T(8,128)(2,1)} %copy_bitcast_fusion.2), calls=%async_computation.1 | async-start | bytes 1048576 | tf_op jit(solution)/shard_map/all_to_all | solution.py:94
  392.1 2.1 select_add_fusion
  394.3 5.6 while.18
  394.9 2.2 bitcast_dynamic-update-slice_fusion.6
  397.7 2.2 bitcast_dynamic-update-slice_fusion.6
  399.9 158.6 %custom-call.4 = f32[8,2,128,128]{2,3,1,0:T(8,128)} custom-call(f32[8,2,128,128]{3,2,1,0:T(8,128)} %bitcast.294), custom_call_target="InvertDiagBlocksLowerTriangular" | custom-call | tf_op jit(solution)/shard_map/jit(_solve_triangular)/vmap()/triangular_solve | solution.py:139
  564.4 2.9 convolution_bitcast_fusion.3
  567.4 2.9 fusion.22
  570.3 31.5 %while.17 = (s32[]{:T(128)}, f32[1,128,128]{1,2,0:T(8,128)S(1)}, f32[1,128,128]{1,2,0:T(8,128)S(1)}, f32[8,1,128,128]{2,3,1,0:T(8,128)}, f32[8,1,128,128]{2,3,1,...) while((s32[]{:T(128)}, f32[1,128,128]{1,2,0:T(8,128)S(1)}, ...), condition=%wide.region_5.6_spmd, body=%wide.region_4.5_spmd.sunk | while | flops 50348032 | bytes 1245293 | solution.py:159
  571.9 1.1 fusion.189
  573.0 1.1 convolution_bitcast_fusion.7
  575.8 1.1 fusion.189
  577.0 1.1 convolution_bitcast_fusion.7
  580.9 1.1 convolution_bitcast_fusion.7
  584.8 1.1 convolution_bitcast_fusion.7
  587.6 1.1 fusion.189
  588.7 1.1 convolution_bitcast_fusion.7
  592.6 1.1 convolution_bitcast_fusion.7
  596.6 1.1 convolution_bitcast_fusion.7
  600.5 1.1 convolution_bitcast_fusion.7
  601.9 1.9 all-gather
  605.3 12.5 %all-gather.1 = f32[512,128]{1,0:T(8,128)S(1)} all-gather(f32[128,128]{1,0:T(8,128)S(1)} %fusion.92), channel_id=3, replica_groups=mesh['tm_0'=4,'tm_1'=4,'tm_2'=2,'stream'=16] {'tm_1'}, dimensions={0}, use_global_device_ids=true | all-gather | bytes 327680 | tf_op jit(solution)/shard_map/all_gather | solution.py:34
  619.9 2.2 all-gather.3
  623.6 12.7 %all-gather.2 = f32[512,128]{1,0:T(8,128)S(1)} all-gather(f32[128,128]{1,0:T(8,128)S(1)} %fusion.98), channel_id=4, replica_groups=mesh['tm_0'=4,'tm_1'=4,'tm_2'=2,'stream'=16] {'tm_0'}, dimensions={0}, use_global_device_ids=true | all-gather | bytes 327680 | tf_op jit(solution)/shard_map/all_gather | solution.py:34
  637.4 12.3 %all-gather.4 = f32[512,128]{1,0:T(8,128)S(1)} all-gather(f32[128,128]{1,0:T(8,128)S(1)} %convolution_add_fusion.7), channel_id=6, replica_groups=mesh['tm_0'=4,'tm_1'=4,'tm_2'=2,'stream'=16] {'tm_1'}, dimensions={0}, use_global_device_ids=true | all-gather | bytes 327680 | tf_op jit(solution)/shard_map/all_gather | solution.py:34
  651.1 12.3 %all-gather.5 = f32[512,128]{1,0:T(8,128)S(1)} all-gather(f32[128,128]{1,0:T(8,128)S(1)} %convolution_add_fusion.4), channel_id=7, replica_groups=mesh['tm_0'=4,'tm_1'=4,'tm_2'=2,'stream'=16] {'tm_0'}, dimensions={0}, use_global_device_ids=true | all-gather | bytes 327680 | tf_op jit(solution)/shard_map/all_gather | solution.py:34
  666.3 2.0 fusion.17
  668.4 1.6 fusion.145
  670.0 2.2 fusion.47
  672.2 3.3 fusion.18
  675.5 12.0 %all-to-all-start.5 = ((bf16[16,128,128]{2,1,0:T(8,128)(2,1)}), bf16[16,128,128]{2,1,0:T(8,128)(2,1)S(1)}, u32[]{:S(2)}, u32[]{:S(2)}) async-start(bf16[16,128,128]{2,1,0:T(8,128)(2,1)} %bitcast.59), calls=%async_computation.5 | async-start | bytes 1048576 | tf_op jit(solution)/shard_map/all_to_all | solution.py:175
  687.6 21.5 %all-to-all-done.5 = bf16[16,128,128]{2,1,0:T(8,128)(2,1)S(1)} async-done(((bf16[16,128,128]{2,1,0:T(8,128)(2,1)}), bf16[16,128,128]{2,1,0:T(8,128)(2,1)S(1)}, u32[]{:S(2)}, u32[]{:S(2)}) %all-to-all-start.5) | async-done | bytes 524320 | tf_op jit(solution)/shard_map/all_to_all | solution.py:175
  709.4 1.1 fusion.40
  (178 shorter events, 47.6 us)
Async XLA Ops:
  6.5 37.8 %copy-start = (bf16[128,2048]{1,0:T(8,128)(2,1)S(1)}, bf16[128,2048]{1,0:T(8,128)(2,1)}, u32[]{:S(2)}) copy-start(bf16[128,2048]{1,0:T(8,128)(2,1)} %param.11) | copy-start | bytes 1572868
  6.5 48.7 %copy-start.21 = (f32[16]{0:T(128)S(1)}, f32[16]{0:T(128)}, u32[]{:S(2)}) copy-start(f32[16]{0:T(128)} %param.18) | copy-start | bytes 196
  6.5 111.9 %all-gather.14.cloned.1.call-start = ((), (), s32[]{:S(2)}) async-start(), calls=%async_computation.8 | async-start | bytes 8912896 | tf_op jit(solution)/shard_map/all_gather | solution.py:71
  7.3 237.8 %all-gather.12.cloned.1.call-start = ((), (), s32[]{:S(2)}) async-start(), calls=%async_computation.7 | async-start | bytes 8912896 | tf_op jit(solution)/shard_map/all_gather | solution.py:70
  8.0 364.6 %all-gather.10.cloned.1.call-start = ((), (), s32[]{:S(2)}) async-start(), calls=%async_computation.6 | async-start | bytes 8912896 | tf_op jit(solution)/shard_map/all_gather | solution.py:69
  45.2 20.2 %all-to-all-start = ((bf16[128,16,1]{0,2,1:T(2,128)(2,1)}), bf16[128,16,1]{0,2,1:T(2,128)(2,1)S(1)}, u32[]{:S(2)}, u32[]{:S(2)}) async-start(bf16[128,16,1]{0,2,1:T(2,128)(2,1)} %copy.65), calls=%async_computation | async-start | bytes 16384 | tf_op jit(solution)/shard_map/all_to_all | solution.py:97
  54.3 337.8 %copy-start.15 = (pred[256,256]{1,0:T(8,128)(4,1)}, pred[256,256]{1,0:T(8,128)(4,1)S(1)}, u32[]{:S(2)}) copy-start(pred[256,256]{1,0:T(8,128)(4,1)S(1)} %iota_compare_fusion.2) | copy-start | bytes 196612
  65.4 58.6 %all-to-all-start.2 = ((bf16[128,16,1]{0,2,1:T(2,128)(2,1)}), bf16[128,16,1]{0,2,1:T(2,128)(2,1)S(1)}, u32[]{:S(2)}, u32[]{:S(2)}) async-start(bf16[128,16,1]{0,2,1:T(2,128)(2,1)} %copy.68), calls=%async_computation.2 | async-start | bytes 16384 | tf_op jit(solution)/shard_map/all_to_all | solution.py:98
  124.0 127.9 %all-to-all-start.4 = ((bf16[128,16,128]{2,0,1:T(8,128)(2,1)}), bf16[128,16,128]{2,0,1:T(8,128)(2,1)S(1)}, u32[]{:S(2)}, u32[]{:S(2)}) async-start(bf16[128,16,128]{2,0,1:T(8,128)(2,1)} %bitcast.256), calls=%async_computation.4 | async-start | bytes 1048576 | tf_op jit(solution)/shard_map/all_to_all | solution.py:96
  251.9 125.4 %copy-start.5 = (bf16[128,16,128]{2,0,1:T(8,128)(2,1)}, bf16[128,16,128]{2,0,1:T(8,128)(2,1)S(1)}, u32[]{:S(2)}) copy-start(bf16[128,16,128]{2,0,1:T(8,128)(2,1)S(1)} %all-to-all-done.4) | copy-start | bytes 1572868
  251.9 129.1 %all-to-all-start.3 = ((bf16[128,16,128]{2,0,1:T(8,128)(2,1)}), bf16[128,16,128]{2,0,1:T(8,128)(2,1)S(1)}, u32[]{:S(2)}, u32[]{:S(2)}) async-start(bf16[128,16,128]{2,0,1:T(8,128)(2,1)} %copy_bitcast_fusion.1), calls=%async_computation.3 | async-start | bytes 1048576 | tf_op jit(solution)/shard_map/all_to_all | solution.py:95
  377.9 1.6 copy-start.6
  379.5 12.6 %copy-start.17 = (pred[256,256]{1,0:T(8,128)(4,1)S(1)}, pred[256,256]{1,0:T(8,128)(4,1)}, u32[]{:S(2)}) copy-start(pred[256,256]{1,0:T(8,128)(4,1)} %get-tuple-element.118) | copy-start | bytes 196612
  380.9 287.4 %all-to-all-start.1 = ((bf16[128,16,128]{2,0,1:T(8,128)(2,1)}), bf16[128,16,128]{2,0,1:T(8,128)(2,1)}, u32[]{:S(2)}, u32[]{:S(2)}) async-start(bf16[128,16,128]{2,0,1:T(8,128)(2,1)} %copy_bitcast_fusion.2), calls=%async_computation.1 | async-start | bytes 1048576 | tf_op jit(solution)/shard_map/all_to_all | solution.py:94
  558.5 1.2 copy-start.3
  559.8 1.2 copy-start.8
  603.8 0.8 copy-start.7
  604.6 0.6 copy-start.10
  605.3 18.3 %copy-start.9 = (f32[128,128]{1,0:T(8,128)}, f32[128,128]{1,0:T(8,128)S(1)}, u32[]{:S(2)}) copy-start(f32[128,128]{1,0:T(8,128)S(1)} %fusion.92) | copy-start | bytes 196612
  619.9 31.0 %copy-start.11 = (f32[128,128]{1,0:T(8,128)S(1)}, f32[128,128]{1,0:T(8,128)}, u32[]{:S(2)}) copy-start(f32[128,128]{1,0:T(8,128)} %copy-done.10) | copy-start | bytes 196612
  619.9 44.2 %copy-start.12 = (f32[128,128]{1,0:T(8,128)S(1)}, f32[128,128]{1,0:T(8,128)}, u32[]{:S(2)}) copy-start(f32[128,128]{1,0:T(8,128)} %fusion.88) | copy-start | bytes 196612
  622.1 42.4 %copy-start.19 = (f32[128]{0:T(128)S(1)}, f32[128]{0:T(128)}, u32[]{:S(2)}) copy-start(f32[128]{0:T(128)} %multiply_reduce_fusion.1) | copy-start | bytes 1540
  623.4 41.3 %copy-start.18 = (f32[128]{0:T(128)S(1)}, f32[128]{0:T(128)}, u32[]{:S(2)}) copy-start(f32[128]{0:T(128)} %multiply_reduce_fusion) | copy-start | bytes 1540
  623.6 41.3 %copy-start.13 = (f32[8,1,128,128]{2,3,1,0:T(8,128)S(1)}, f32[8,1,128,128]{2,3,1,0:T(8,128)}, u32[]{:S(2)}) copy-start(f32[8,1,128,128]{2,3,1,0:T(8,128)} %get-tuple-element.48) | copy-start | bytes 1572868
  623.6 41.3 %copy-start.14 = (f32[8,1,128,128]{2,3,1,0:T(8,128)S(1)}, f32[8,1,128,128]{2,3,1,0:T(8,128)}, u32[]{:S(2)}) copy-start(f32[8,1,128,128]{2,3,1,0:T(8,128)} %get-tuple-element.45) | copy-start | bytes 1572868
  665.5 0.8 copy-start.1
  668.4 1.6 copy-start.2
  668.4 3.8 copy-start.4
  668.4 3.9 copy-start.16
  672.2 15.3 %copy-start.20 = (f32[128]{0:T(128)S(1)}, f32[128]{0:T(128)}, u32[]{:S(2)}) copy-start(f32[128]{0:T(128)} %param.19) | copy-start | bytes 1540
  675.5 33.5 %all-to-all-start.5 = ((bf16[16,128,128]{2,1,0:T(8,128)(2,1)}), bf16[16,128,128]{2,1,0:T(8,128)(2,1)S(1)}, u32[]{:S(2)}, u32[]{:S(2)}) async-start(bf16[16,128,128]{2,1,0:T(8,128)(2,1)} %bitcast.59), calls=%async_computation.5 | async-start | bytes 1048576 | tf_op jit(solution)/shard_map/all_to_all | solution.py:175
Sparse Core Ops, SparseCore 0:
  9.4 108.9 all-gather.13
  120.5 124.5 all-gather.11
  247.1 125.4 all-gather.9
where the time goes:
time: 719 us; the launch traced here: 717 us
  waiting for transfers between devices  299 us (42%)
  other arithmetic  171 us (24%)
  blocking collectives  88 us (12%)
  matrix products  59.8 us (8%)
  starting transfers between devices  59.5 us (8%)
  local copies, waits for them, and re-layouts  26.1 us (4%)
  between operations  13.7 us (2%)
    another operation x3, other arithmetic, shards(): jax.scipy.linalg.solve_triangular(lower, right_side, lower=True, unit_dia...  159 us
    all_gather x1, waiting for transfers between devices, shards(): raw_key = fold_one(lax.all_gather(w_key, 'stream', axis=0, tiled=True))  109 us
    all_gather x1, waiting for transfers between devices, shards(): raw_query = fold_one(lax.all_gather(w_query, 'stream', axis=0, tiled=True))  109 us
    all_gather x6, blocking collectives, carried_in(): pieces = jax.tree.map(lambda part: lax.all_gather(part, axis), subtotal)  53.8 us
    all_gather x1, waiting for transfers between devices, shards(): raw_value = fold_one(lax.all_gather(w_value, 'stream', axis=0, tiled=True))  47.6 us
    all_gather x1, blocking collectives, in_one_piece(): whole = lax.all_gather(both, axis, axis=dim, tiled=True)  34.2 us
    all_to_all x1, waiting for transfers between devices, shards(): lax.all_to_all(readout, 'stream', split_axis=0, concat_axis=1, tiled=True)  21.5 us
    dot_general x5, matrix products, add_rows(): return jnp.dot(inputs, piece, preferred_element_type=jnp.float32)  14.4 us
  transfers between devices with their start and end apart: 9, of which 5 were waited for; matrix products, arithmetic and copies ran while one was open for 34% of the time, Pallas kernels for 0%

commit v1 on v0

--- a/solution.py
+++ b/solution.py
@@ -68,7 +68,11 @@
 
     raw_query = fold_one(lax.all_gather(w_query, "stream", axis=0, tiled=True))
     raw_key = fold_one(lax.all_gather(w_key, "stream", axis=0, tiled=True))
-    raw_value = fold_one(lax.all_gather(w_value, "stream", axis=0, tiled=True))
+    raw_value = fold_one(
+        jnp.concatenate(
+            lax.all_to_all(jnp.stack([w_value] * lax.axis_size("stream")), "stream", 0, 0), axis=0
+        )
+    )
     pieces = in_one_piece((decay_proj, beta_proj), "stream", 0, 1)
     decay_logit, beta_logit = tuple((add_rows(tokens, piece) for piece in pieces))
     query_heads = raw_query.reshape(local_rows, HEADS, DK)

time: 719 us -> 1010 us (1.40)
  waiting for transfers between devices: 299 us -> 563 us
  blocking collectives: 88 us -> 120 us
    all_gather x1, waiting for transfers between devices: 109 us -> 446 us  [shards(): raw_query = fold_one(lax.all_gather(w_query, 'stream', axis=0, tiled=True))]
    all_gather x1 -> x0, waiting for transfers between devices: 47.6 us -> none  [shards(): raw_value = fold_one(lax.all_gather(w_value, 'stream', axis=0, tiled=True))]
    all_gather x1, waiting for transfers between devices: 109 us -> 63.7 us  [shards(): raw_key = fold_one(lax.all_gather(w_key, 'stream', axis=0, tiled=True))]
    all_to_all x0 -> x1, blocking collectives: none -> 31.5 us  [shards(): lax.all_to_all(key_rows, 'stream', split_axis=1, concat_axis=0, tiled=True)]
    all_to_all x1, waiting for transfers between devices: 0.01 us -> 21.2 us  [shards(): lax.all_to_all(queries, 'stream', split_axis=1, concat_axis=0, tiled=True)]
    all_to_all x1, waiting for transfers between devices: 0.01 us -> 10.3 us  [shards(): lax.all_to_all(strength, 'stream', split_axis=1, concat_axis=0, tiled=True)]
  transfers between devices with their start and end apart: 9 -> 8, of which waited for: 5 -> 5; matrix products, arithmetic and copies ran while one was open for 34% -> 19% of each run, Pallas kernels for 0% -> 0%
where the time goes in v1:
time: 1010 us
  waiting for transfers between devices  563 us (56%)
  other arithmetic  169 us (17%)
  blocking collectives  120 us (12%)
  starting transfers between devices  57 us (6%)
  matrix products  54.7 us (5%)
  local copies, waits for them, and re-layouts  27.6 us (3%)
  between operations  14.1 us (1%)
    all_gather x1, waiting for transfers between devices, shards(): raw_query = fold_one(lax.all_gather(w_query, 'stream', axis=0, tiled=True))  446 us
    another operation x3, other arithmetic, shards(): jax.scipy.linalg.solve_triangular(lower, right_side, lower=True, unit_dia...  159 us
    all_gather x1, waiting for transfers between devices, shards(): raw_key = fold_one(lax.all_gather(w_key, 'stream', axis=0, tiled=True))  63.7 us
    all_gather x6, blocking collectives, carried_in(): pieces = jax.tree.map(lambda part: lax.all_gather(part, axis), subtotal)  54 us
    all_gather x1, blocking collectives, in_one_piece(): whole = lax.all_gather(both, axis, axis=dim, tiled=True)  34.3 us
    all_to_all x1, blocking collectives, shards(): lax.all_to_all(key_rows, 'stream', split_axis=1, concat_axis=0, tiled=True)  31.5 us
    all_to_all x1, waiting for transfers between devices, shards(): lax.all_to_all(queries, 'stream', split_axis=1, concat_axis=0, tiled=True)  21.2 us
    all_to_all x1, waiting for transfers between devices, shards(): lax.all_to_all(readout, 'stream', split_axis=0, concat_axis=1, tiled=True)  20.2 us
  transfers between devices with their start and end apart: 8, of which 5 were waited for; matrix products, arithmetic and copies ran while one was open for 19% of the time, Pallas kernels for 0%

profile of v1, /device:TPU:34, one launch (start us, length us, event | category | flops | bytes accessed | tf_op | source)
XLA Modules:
  0.0 1005.4 jit_solution(14704860400169249311)
XLA Ops:
  8.6 34.3 %all_gather.45 = bf16[2048,32]{0,1:T(8,128)(2,1)S(1)} all-gather(bf16[128,32]{0,1:T(8,128)(2,1)S(1)} %pad_maximum_fusion), channel_id=1, replica_groups=mesh['tm_0'=4,'tm_1'=4,'tm_2'=2,'stream'=16] {'stream'}, dimensions={0}, use_global_device_ids=true | all-gather | bytes 139264 | tf_op jit(solution)/shard_map/all_gather | solution.py:19
  43.8 8.9 all-to-all-start
  54.1 63.7 %all-gather.11.cloned.1.call-done = bf16[2048,2048]{1,0:T(8,128)(2,1)} async-done(((bf16[128,2048]{1,0:T(8,128)(2,1)}), bf16[2048,2048]{1,0:T(8,128)(2,1)}) %all-gather.11.cloned.1.call-update) | async-done | bytes 8388624 | tf_op jit(solution)/shard_map/all_gather | solution.py:70
  117.9 4.6 fusion.143
  123.2 11.5 %all-to-all-start.2 = ((bf16[128,16,1]{0,2,1:T(2,128)(2,1)}), bf16[128,16,1]{0,2,1:T(2,128)(2,1)S(1)}, u32[]{:S(2)}, u32[]{:S(2)}) async-start(bf16[128,16,1]{0,2,1:T(2,128)(2,1)} %copy.68), calls=%async_computation.2 | async-start | bytes 16384 | tf_op jit(solution)/shard_map/all_to_all | solution.py:102
  135.4 10.3 %all-to-all-done.2 = bf16[128,16,1]{0,2,1:T(2,128)(2,1)S(1)} async-done(((bf16[128,16,1]{0,2,1:T(2,128)(2,1)}), bf16[128,16,1]{0,2,1:T(2,128)(2,1)S(1)}, u32[]{:S(2)}, u32[]{:S(2)}) %all-to-all-start.2) | async-done | bytes 4128 | tf_op jit(solution)/shard_map/all_to_all | solution.py:102
  145.8 31.5 %all_to_all.86 = bf16[128,16,128]{2,0,1:T(8,128)(2,1)S(1)} all-to-all(bf16[128,16,128]{2,0,1:T(8,128)(2,1)S(1)} %copy_bitcast_fusion.1), channel_id=1, replica_groups=mesh['tm_0'=4,'tm_1'=4,'tm_2'=2,'stream'=16] {'stream'}, dimensions={1} | all-to-all | bytes 1048576 | tf_op jit(solution)/shard_map/all_to_all | solution.py:99
  177.2 4.3 stack.2
  181.5 6.7 all-to-all-start.4
  189.0 445.6 %all-gather.9.cloned.1.call-done = bf16[2048,2048]{1,0:T(8,128)(2,1)} async-done(((bf16[128,2048]{1,0:T(8,128)(2,1)}), bf16[2048,2048]{1,0:T(8,128)(2,1)}) %all-gather.9.cloned.1.call-update) | async-done | bytes 8388624 | tf_op jit(solution)/shard_map/all_gather | solution.py:69
  634.7 4.6 fusion.142
  640.3 1.2 copy_bitcast_fusion.2
  641.5 11.0 %all-to-all-start.1 = ((bf16[128,16,128]{2,0,1:T(8,128)(2,1)}), bf16[128,16,128]{2,0,1:T(8,128)(2,1)S(1)}, u32[]{:S(2)}, u32[]{:S(2)}) async-start(bf16[128,16,128]{2,0,1:T(8,128)(2,1)} %copy_bitcast_fusion.2), calls=%async_computation.1 | async-start | bytes 1048576 | tf_op jit(solution)/shard_map/all_to_all | solution.py:98
  654.5 4.7 fusion.21
  660.1 21.2 %all-to-all-done.1 = bf16[128,16,128]{2,0,1:T(8,128)(2,1)S(1)} async-done(((bf16[128,16,128]{2,0,1:T(8,128)(2,1)}), bf16[128,16,128]{2,0,1:T(8,128)(2,1)S(1)}, u32[]{:S(2)}, u32[]{:S(2)}) %all-to-all-start.1) | async-done | bytes 524320 | tf_op jit(solution)/shard_map/all_to_all | solution.py:98
  681.3 6.8 all-to-all-start.5
  689.6 5.6 while.18
  690.2 2.2 bitcast_dynamic-update-slice_fusion.6
  693.0 2.2 bitcast_dynamic-update-slice_fusion.6
  695.2 158.6 %custom-call.4 = f32[8,2,128,128]{2,3,1,0:T(8,128)} custom-call(f32[8,2,128,128]{3,2,1,0:T(8,128)} %bitcast.297), custom_call_target="InvertDiagBlocksLowerTriangular" | custom-call | tf_op jit(solution)/shard_map/jit(_solve_triangular)/vmap()/triangular_solve | solution.py:143
  853.9 1.3 convert_multiply_fusion.1
  855.2 1.8 fusion.145
  857.0 1.2 convert_element_type.187
  863.2 2.9 convolution_bitcast_fusion.3
  866.2 2.9 fusion.22
  869.1 31.3 %while.17 = (s32[]{:T(128)}, f32[1,128,128]{1,2,0:T(8,128)S(1)}, f32[1,128,128]{1,2,0:T(8,128)S(1)}, f32[8,1,128,128]{2,3,1,0:T(8,128)}, f32[8,1,128,128]{2,3,1,...) while((s32[]{:T(128)}, f32[1,128,128]{1,2,0:T(8,128)S(1)}, ...), condition=%wide.region_5.6_spmd, body=%wide.region_4.5_spmd.sunk | while | flops 50348032 | bytes 1246809 | solution.py:163
  870.7 1.1 fusion.189
  871.8 1.1 convolution_bitcast_fusion.7
  874.6 1.1 fusion.189
  875.8 1.1 convolution_bitcast_fusion.7
  878.5 1.1 fusion.189
  882.5 1.1 fusion.189
  883.6 1.1 convolution_bitcast_fusion.7
  886.4 1.1 fusion.189
  890.3 1.1 fusion.189
  894.2 1.1 fusion.189
  898.1 1.1 fusion.189
  900.5 1.9 all-gather
  902.8 12.5 %all-gather.1 = f32[512,128]{1,0:T(8,128)S(1)} all-gather(f32[128,128]{1,0:T(8,128)S(1)} %fusion.92), channel_id=3, replica_groups=mesh['tm_0'=4,'tm_1'=4,'tm_2'=2,'stream'=16] {'tm_1'}, dimensions={0}, use_global_device_ids=true | all-gather | bytes 327680 | tf_op jit(solution)/shard_map/all_gather | solution.py:34
  915.7 1.9 all-gather.3
  917.8 12.3 %all-gather.4 = f32[512,128]{1,0:T(8,128)S(1)} all-gather(f32[128,128]{1,0:T(8,128)S(1)} %convolution_add_fusion.7), channel_id=6, replica_groups=mesh['tm_0'=4,'tm_1'=4,'tm_2'=2,'stream'=16] {'tm_1'}, dimensions={0}, use_global_device_ids=true | all-gather | bytes 327680 | tf_op jit(solution)/shard_map/all_gather | solution.py:34
  931.4 12.9 %all-gather.2 = f32[512,128]{1,0:T(8,128)S(1)} all-gather(f32[128,128]{1,0:T(8,128)S(1)} %fusion.98), channel_id=4, replica_groups=mesh['tm_0'=4,'tm_1'=4,'tm_2'=2,'stream'=16] {'tm_0'}, dimensions={0}, use_global_device_ids=true | all-gather | bytes 327680 | tf_op jit(solution)/shard_map/all_gather | solution.py:34
  944.9 12.5 %all-gather.5 = f32[512,128]{1,0:T(8,128)S(1)} all-gather(f32[128,128]{1,0:T(8,128)S(1)} %convolution_add_fusion.4), channel_id=7, replica_groups=mesh['tm_0'=4,'tm_1'=4,'tm_2'=2,'stream'=16] {'tm_0'}, dimensions={0}, use_global_device_ids=true | all-gather | bytes 327680 | tf_op jit(solution)/shard_map/all_gather | solution.py:34
  960.2 1.2 fusion.47
  961.5 3.3 fusion.18
  964.8 12.0 %all-to-all-start.6 = ((bf16[16,128,128]{2,1,0:T(8,128)(2,1)}), bf16[16,128,128]{2,1,0:T(8,128)(2,1)S(1)}, u32[]{:S(2)}, u32[]{:S(2)}) async-start(bf16[16,128,128]{2,1,0:T(8,128)(2,1)} %bitcast.60), calls=%async_computation.6 | async-start | bytes 1048576 | tf_op jit(solution)/shard_map/all_to_all | solution.py:179
  976.8 20.2 %all-to-all-done.6 = bf16[16,128,128]{2,1,0:T(8,128)(2,1)S(1)} async-done(((bf16[16,128,128]{2,1,0:T(8,128)(2,1)}), bf16[16,128,128]{2,1,0:T(8,128)(2,1)S(1)}, u32[]{:S(2)}, u32[]{:S(2)}) %all-to-all-start.6) | async-done | bytes 524320 | tf_op jit(solution)/shard_map/all_to_all | solution.py:179
  997.4 1.1 fusion.40
  (161 shorter events, 42.4 us)
Async XLA Ops:
  6.5 36.3 %copy-start = (bf16[128,2048]{1,0:T(8,128)(2,1)S(1)}, bf16[128,2048]{1,0:T(8,128)(2,1)}, u32[]{:S(2)}) copy-start(bf16[128,2048]{1,0:T(8,128)(2,1)} %param.11) | copy-start | bytes 1572868
  6.5 111.3 %all-gather.11.cloned.1.call-start = ((), (), s32[]{:S(2)}) async-start(), calls=%async_computation.8 | async-start | bytes 8912896 | tf_op jit(solution)/shard_map/all_gather | solution.py:70
  43.8 79.4 %all-to-all-start = ((bf16[128,16,1]{0,2,1:T(2,128)(2,1)}), bf16[128,16,1]{0,2,1:T(2,128)(2,1)S(1)}, u32[]{:S(2)}, u32[]{:S(2)}) async-start(bf16[128,16,1]{0,2,1:T(2,128)(2,1)} %copy.65), calls=%async_computation | async-start | bytes 16384 | tf_op jit(solution)/shard_map/all_to_all | solution.py:101
  123.2 22.6 %all-to-all-start.2 = ((bf16[128,16,1]{0,2,1:T(2,128)(2,1)}), bf16[128,16,1]{0,2,1:T(2,128)(2,1)S(1)}, u32[]{:S(2)}, u32[]{:S(2)}) async-start(bf16[128,16,1]{0,2,1:T(2,128)(2,1)} %copy.68), calls=%async_computation.2 | async-start | bytes 16384 | tf_op jit(solution)/shard_map/all_to_all | solution.py:102
  135.0 42.2 %copy-start.8 = (bf16[128,2048]{1,0:T(8,128)(2,1)S(1)}, bf16[128,2048]{1,0:T(8,128)(2,1)}, u32[]{:S(2)}) copy-start(bf16[128,2048]{1,0:T(8,128)(2,1)} %param.14) | copy-start | bytes 1572868
  181.5 460.0 %all-to-all-start.4 = ((bf16[16,128,2048]{2,1,0:T(8,128)(2,1)}), bf16[16,128,2048]{2,1,0:T(8,128)(2,1)}, u32[]{:S(2)}, u32[]{:S(2)}) async-start(bf16[16,128,2048]{2,1,0:T(8,128)(2,1)} %stack.2), calls=%async_computation.4 | async-start | bytes 16777216 | tf_op jit(solution)/shard_map/all_to_all | solution.py:73
  188.2 446.4 %all-gather.9.cloned.1.call-start = ((), (), s32[]{:S(2)}) async-start(), calls=%async_computation.7 | async-start | bytes 8912896 | tf_op jit(solution)/shard_map/all_gather | solution.py:69
  641.5 39.8 %all-to-all-start.1 = ((bf16[128,16,128]{2,0,1:T(8,128)(2,1)}), bf16[128,16,128]{2,0,1:T(8,128)(2,1)S(1)}, u32[]{:S(2)}, u32[]{:S(2)}) async-start(bf16[128,16,128]{2,0,1:T(8,128)(2,1)} %copy_bitcast_fusion.2), calls=%async_computation.1 | async-start | bytes 1048576 | tf_op jit(solution)/shard_map/all_to_all | solution.py:98
  659.1 29.3 %copy-start.11 = (f32[256,256]{1,0:T(8,128)S(1)}, f32[256,256]{1,0:T(8,128)}, u32[]{:S(2)}) copy-start(f32[256,256]{1,0:T(8,128)} %get-tuple-element.119) | copy-start | bytes 786436
  659.1 29.3 %copy-start.12 = (f32[256,256]{1,0:T(8,128)S(1)}, f32[256,256]{1,0:T(8,128)}, u32[]{:S(2)}) copy-start(f32[256,256]{1,0:T(8,128)} %get-tuple-element.120) | copy-start | bytes 786436
  681.3 7.1 copy-start.3
  681.3 175.7 %all-to-all-start.5 = ((bf16[128,16,128]{2,0,1:T(8,128)(2,1)}), bf16[128,16,128]{2,0,1:T(8,128)(2,1)}, u32[]{:S(2)}, u32[]{:S(2)}) async-start(bf16[128,16,128]{2,0,1:T(8,128)(2,1)} %bitcast.257), calls=%async_computation.5 | async-start | bytes 1048576 | tf_op jit(solution)/shard_map/all_to_all | solution.py:100
  689.6 165.6 %copy-start.4 = (bf16[128,16,128]{2,0,1:T(8,128)(2,1)S(1)}, bf16[128,16,128]{2,0,1:T(8,128)(2,1)}, u32[]{:S(2)}) copy-start(bf16[128,16,128]{2,0,1:T(8,128)(2,1)} %copy-done.3) | copy-start | bytes 1572868
  857.0 1.6 copy-start.6
  858.5 1.2 copy-start.7
  930.3 28.2 %copy-start.9 = (f32[8,1,128,128]{2,3,1,0:T(8,128)S(1)}, f32[8,1,128,128]{2,3,1,0:T(8,128)}, u32[]{:S(2)}) copy-start(f32[8,1,128,128]{2,3,1,0:T(8,128)} %get-tuple-element.45) | copy-start | bytes 1572868
  930.3 28.2 %copy-start.10 = (f32[8,1,128,128]{2,3,1,0:T(8,128)S(1)}, f32[8,1,128,128]{2,3,1,0:T(8,128)}, u32[]{:S(2)}) copy-start(f32[8,1,128,128]{2,3,1,0:T(8,128)} %get-tuple-element.48) | copy-start | bytes 1572868
  958.5 1.7 copy-start.5
  959.1 2.3 copy-start.2
  961.4 15.4 %copy-start.13 = (f32[128]{0:T(128)S(1)}, f32[128]{0:T(128)}, u32[]{:S(2)}) copy-start(f32[128]{0:T(128)} %param.19) | copy-start | bytes 1540
  961.5 37.1 %copy-start.1 = (bf16[128,2048]{1,0:T(8,128)(2,1)S(1)}, bf16[128,2048]{1,0:T(8,128)(2,1)}, u32[]{:S(2)}) copy-start(bf16[128,2048]{1,0:T(8,128)(2,1)} %param.11) | copy-start | bytes 1572868
  964.8 32.3 %all-to-all-start.6 = ((bf16[16,128,128]{2,1,0:T(8,128)(2,1)}), bf16[16,128,128]{2,1,0:T(8,128)(2,1)S(1)}, u32[]{:S(2)}, u32[]{:S(2)}) async-start(bf16[16,128,128]{2,1,0:T(8,128)(2,1)} %bitcast.60), calls=%async_computation.6 | async-start | bytes 1048576 | tf_op jit(solution)/shard_map/all_to_all | solution.py:179
Sparse Core Ops, SparseCore 0:
  9.4 108.3 all-gather.10
  191.1 443.4 all-gather.8
